TPU v7x, 128 devices: a whole 4x4x4 slice. The times are simulated.
128 devices in a mesh: tm: 4 (over x_hi, core), space: 32 (over y, x_lo, z).
Axes of the slice: x: 4 (x_hi: 2, x_lo: 2; x = x_hi * 2 + x_lo), y: 4, z: 4, core: 2. Of those that a mesh axis runs over, the one named last changes fastest.
Arguments:
- states: float32 [8, 3, 128, 128, 128], P('tm', None, 'space'), may hold values from -6 to 6
- sources: float32 [8, 3, 128, 128, 128], P('tm', None, 'space'), may hold values from -6 to 6
- conductivity: float32 [128, 128, 128], P('space'), may hold values from 0.5 to 4
- gap_tile: int32 [8, 4096, 1], P('tm', 'space'), may hold values from 0 to 31; in each aligned block of 128 rows (0 to 127, 128 to 255, ..., all dimensions but the last counted through in order) at most 8 rows name the same one
- gap_row: int32 [8, 4096], P('tm', 'space'), may hold values from 0 to 127
Outputs:
- new_states: float32 [8, 3, 128, 128, 128], P('tm', None, 'space')
Inputs may be any that keep to these rules, and one draw needn't show every extreme that they name: `gap_tile`: in each slice no tile maps more than 8 of its own 128 interface rows to any one tile.
All inputs are finite; a program needn't handle non-finite values.
Results may differ from a plain program's by a relative error of at most 0.0001.
Values sent between devices are 32-bit elements; how exact they have to be, the bound alone decides.
A program may use at most 128 MiB of HBM per device.

v0:
```python
import jax
import jax.numpy as jnp
from jax import lax
from jax.sharding import PartitionSpec as P

STEPS = 4
SWEEPS = 3
COARSE_SWEEPS = 3


inverse_step = 2.0
gap_gain = 1.0


def padded_2(cells, sides, width):
    for axis, dim in sides:
        count = lax.axis_size(axis)
        ends = count - 1
        head = lax.slice_in_dim(cells, 0, width, axis=dim)
        tail = lax.slice_in_dim(cells, cells.shape[dim] - width, cells.shape[dim], axis=dim)
        cells = jnp.concatenate(
            [
                lax.ppermute(tail, axis, [(i, (i + 1) % count) for i in range(ends)]),
                cells,
                lax.ppermute(head, axis, [((i + 1) % count, i) for i in range(ends)]),
            ],
            axis=dim,
        )
    return cells


def passed_along(value, axis, steps):
    count = lax.axis_size(axis)
    pairs = [(source, (source + steps) % count) for source in range(count)]
    return lax.ppermute(value, axis, pairs)


def passed_along_2(value, axis, steps):
    count = lax.axis_size(axis)
    first, last = (max(0, -steps), min(count, count - steps))
    return lax.ppermute(value, axis, [(source, source + steps) for source in range(first, last)])


def neighbours(field):
    wide = padded_2(field, (("space", 2),), 1)
    padded = jnp.pad(wide, ((0, 0), (0, 0), (0, 0), (1, 1), (1, 1)))
    total = padded[:, :, 2:, 1:-1, 1:-1] + padded[:, :, :-2, 1:-1, 1:-1]
    total = total + padded[:, :, 1:-1, 2:, 1:-1] + padded[:, :, 1:-1, :-2, 1:-1]
    total = total + padded[:, :, 1:-1, 1:-1, 2:] + padded[:, :, 1:-1, 1:-1, :-2]
    return total


def jacobi(field, rhs, diag, sweeps):
    for sweep in range(sweeps):
        field = (rhs + neighbours(field)) / diag
    return field


def shards(states, sources, conductivity, gap_tile, gap_row):
    own_tile = lax.axis_index("space")
    rows_count = states.shape[3]
    conduct = conductivity[None, None]
    tiles = gap_tile[:, :, 0]
    row_ids = jnp.arange(rows_count, dtype=jnp.int32)
    all_tiles, all_rows = (
        lax.all_gather(tiles, "space", axis=1, tiled=True),
        lax.all_gather(gap_row, "space", axis=1, tiled=True),
    )
    mine = (
        (all_tiles[:, None, :] == own_tile) & (all_rows[:, None, :] == row_ids[None, :, None])
    ).astype(jnp.float32)
    rate = inverse_step * conduct

    def coarse(field, first, last):
        coarse_rate = inverse_step * conduct / STEPS
        return jacobi(
            field, coarse_rate * field + sources[first:last], coarse_rate + 6.0, COARSE_SWEEPS
        )

    field = states
    for step in range(STEPS):
        every_row = lax.all_gather(field[:, 0, 0], "space", axis=1, tiled=True)
        coupled = jnp.einsum("syr,srz->syz", mine, every_row, precision=lax.Precision.HIGHEST)
        rhs = rate * field + sources
        rhs = rhs.at[:, 0, 0].add(gap_gain * coupled)
        field = jacobi(field, rhs, rate + 6.0, SWEEPS)
    coarse_old = coarse(states, 0, states.shape[0])
    jumps = field - coarse_old
    fine_before = passed_along(field[-1:], "tm", 1)
    incoming = fine_before
    position_tm = lax.axis_index("tm")
    for rounds in range(lax.axis_size("tm") - 1):
        second = coarse(incoming, 0, 1) + jumps[0:1]
        onward = coarse(second, 1, 2) - coarse_old[1:2]
        arrived_state = passed_along_2(onward, "tm", 1)
        incoming = jnp.where(position_tm == rounds + 1, arrived_state + fine_before, incoming)
    second = coarse(incoming, 0, 1) + jumps[0:1]
    return jnp.concatenate([incoming, second], axis=0)


def solution(mesh):
    placed = (
        P("tm", None, "space", None, None),
        P("tm", None, "space", None, None),
        P("space", None, None),
        P("tm", "space", None),
        P("tm", "space"),
    )
    return jax.shard_map(
        shards,
        mesh=mesh,
        in_specs=placed,
        out_specs=P("tm", None, "space", None, None),
        check_vma=False,
    )
```

profile of v0, /device:TPU:13, one launch (start us, length us, event | category | flops | bytes accessed | tf_op | source)
XLA Modules:
  0.0 1236.4 jit_solution(5661439499863379767)
XLA Ops:
  13.7 6.2 collective-permute-start
  21.9 64.0 %all-gather = s32[2,4096,1]{1,2,0:T(1,128)S(1)} all-gather(s32[2,128,1]{1,2,0:T(1,128)S(1)} %copy-done.30), channel_id=2, replica_groups=mesh['tm'=4,'space'=32] {'space'}, dimensions={1}, use_global_device_ids=true | all-gather | bytes 33792 | tf_op jit(solution)/shard_map/all_gather | solution.py:66
  86.0 58.0 %all_gather.19 = s32[2,4096]{1,0:T(2,128)S(1)} all-gather(s32[2,128]{1,0:T(2,128)S(1)} %copy-done.31), channel_id=1, replica_groups=mesh['tm'=4,'space'=32] {'space'}, dimensions={1}, use_global_device_ids=true | all-gather | bytes 33792 | tf_op jit(solution)/shard_map/all_gather | solution.py:67
  154.1 6.3 add_divide_fusion.1
  160.4 6.8 collective-permute-start.2
  172.0 6.8 collective-permute-done.3
  216.2 5.5 collective-permute-done.7
  225.3 138.8 %all-gather.12.cloned.1.call-done = f32[2,1,1,4096,128]{4,3,0,2,1:T(8,128)} async-done(((f32[2,1,1,128,128]{4,3,0,2,1:T(8,128)}), f32[2,1,1,4096,128]{4,3,0,2,1:T(8,128)}) %all-gather.12.cloned.1.call-update) | async-done | bytes 4194320 | tf_op jit(solution)/shard_map/all_gather | solution.py:82
  364.1 5.9 fusion.169
  370.0 6.5 fusion.58
  385.1 5.9 collective-permute-done.9
  404.7 6.7 collective-permute-done.11
  440.3 134.4 %all-gather.14.cloned.1.call-done = f32[2,1,1,4096,128]{4,3,0,2,1:T(8,128)} async-done(((f32[2,1,1,128,128]{4,3,0,2,1:T(8,128)}), f32[2,1,1,4096,128]{4,3,0,2,1:T(8,128)}) %all-gather.14.cloned.1.call-update) | async-done | bytes 4194320 | tf_op jit(solution)/shard_map/all_gather | solution.py:82
  574.7 5.9 fusion.168
  580.6 6.6 fusion.49
  595.9 6.6 collective-permute-done.15
  616.4 6.1 collective-permute-done.17
  651.3 134.6 %all-gather.16.cloned.1.call-done = f32[2,1,1,4096,128]{4,3,0,2,1:T(8,128)} async-done(((f32[2,1,1,128,128]{4,3,0,2,1:T(8,128)}), f32[2,1,1,4096,128]{4,3,0,2,1:T(8,128)}) %all-gather.16.cloned.1.call-update) | async-done | bytes 4194320 | tf_op jit(solution)/shard_map/all_gather | solution.py:82
  785.9 5.9 fusion.167
  791.8 6.6 fusion.40
  807.0 6.6 collective-permute-done.21
  822.5 5.8 collective-permute-start.31
  836.6 23.8 %collective-permute-start.24 = (f32[1,3,4,128,128]{4,3,0,2,1:T(8,128)S(1)}, f32[1,3,4,128,128]{4,3,0,2,1:T(8,128)S(1)}, u32[]{:S(2)}, u32[]{:S(2)}) collective-permute-start(f32[1,3,4,128,128]{4,3,0,2,1:T(8,128)S(1)} %slice.1534), channel_id=1, source_target_pairs={{0,32},{32,64},{64,96},{96,0},{1,33},{33,65},{65,97},{97,1},{2,34}... | collective-permute-start | bytes 2359304 | tf_op jit(solution)/shard_map/ppermute | solution.py:35
  863.8 5.5 collective-permute-done.24
  869.3 5.7 collective-permute-start.25
  877.0 6.4 collective-permute-start.33
  886.9 6.4 collective-permute-start.27
  958.8 12.8 %collective-permute-done.41 = f32[1,3,4,128,128]{4,3,0,2,1:T(8,128)} collective-permute-done((f32[1,3,4,128,128]{4,3,0,2,1:T(8,128)}, f32[1,3,4,128,128]{4,3,0,2,1:T(8,128)}, u32[]{:S(2)}, u32[]{:S(2)}) %collective-permute-start.41) | collective-permute-done | bytes 786464 | tf_op jit(solution)/shard_map/ppermute | solution.py:41
  1055.4 22.3 %collective-permute-done.54 = f32[1,3,4,128,128]{4,3,0,2,1:T(8,128)} collective-permute-done((f32[1,3,4,128,128]{4,3,0,2,1:T(8,128)}, f32[1,3,4,128,128]{4,3,0,2,1:T(8,128)}, u32[]{:S(2)}, u32[]{:S(2)}) %collective-permute-start.54) | collective-permute-done | bytes 786464 | tf_op jit(solution)/shard_map/ppermute | solution.py:41
  1099.0 6.8 collective-permute-done.58
  1163.7 21.3 %collective-permute-done.67 = f32[1,3,4,128,128]{4,3,0,2,1:T(8,128)} collective-permute-done((f32[1,3,4,128,128]{4,3,0,2,1:T(8,128)}, f32[1,3,4,128,128]{4,3,0,2,1:T(8,128)}, u32[]{:S(2)}, u32[]{:S(2)}) %collective-permute-start.67) | collective-permute-done | bytes 786464 | tf_op jit(solution)/shard_map/ppermute | solution.py:41
  1206.6 5.9 collective-permute-done.71
  (317 shorter events, 468.0 us)
Async XLA Ops:
  6.5 142.3 %all-gather.10.cloned.1.call-start = ((), (), s32[]{:S(2)}) async-start(), calls=%async_computation | async-start | bytes 4325376 | tf_op jit(solution)/shard_map/all_gather | solution.py:82
  11.6 352.5 %all-gather.12.cloned.1.call-start = ((), (), s32[]{:S(2)}) async-start(), calls=%async_computation.1 | async-start | bytes 4325376 | tf_op jit(solution)/shard_map/all_gather | solution.py:82
  13.7 130.3 %collective-permute-start = (f32[2,3,1,128,128]{4,3,0,2,1:T(8,128)}, f32[2,3,1,128,128]{4,3,0,2,1:T(8,128)S(1)}, u32[]{:S(2)}, u32[]{:S(2)}) collective-permute-start(f32[2,3,1,128,128]{4,3,0,2,1:T(8,128)} %get-tuple-element.95), channel_id=1, source_target_pairs={{1,0},{2,1},{3,2},{4,3},{5,4},{6,5},{7,6},{8,7},{9,8},{10,9},{11,1... | collective-permute-start | bytes 1179656 | tf_op jit(solution)/shard_map/ppermute | solution.py:25
  19.9 124.1 %collective-permute-start.1 = (f32[2,3,1,128,128]{4,3,0,2,1:T(8,128)}, f32[2,3,1,128,128]{4,3,0,2,1:T(8,128)S(1)}, u32[]{:S(2)}, u32[]{:S(2)}) collective-permute-start(f32[2,3,1,128,128]{4,3,0,2,1:T(8,128)} %get-tuple-element.94), channel_id=1, source_target_pairs={{0,1},{1,2},{2,3},{3,4},{4,5},{5,6},{6,7},{7,8},{8,9},{9,10},{10,1... | collective-permute-start | bytes 1179656 | tf_op jit(solution)/shard_map/ppermute | solution.py:23
  160.4 11.5 collective-permute-start.2
  167.3 11.5 collective-permute-start.3
  185.7 11.8 collective-permute-start.5
  205.1 369.6 %all-gather.14.cloned.1.call-start = ((), (), s32[]{:S(2)}) async-start(), calls=%async_computation.2 | async-start | bytes 4325376 | tf_op jit(solution)/shard_map/all_gather | solution.py:82
  209.4 12.3 collective-permute-start.7
  379.2 11.8 collective-permute-start.9
  398.0 13.5 %collective-permute-start.11 = (f32[2,3,1,128,128]{4,3,0,2,1:T(8,128)S(1)}, f32[2,3,1,128,128]{4,3,0,2,1:T(8,128)S(1)}, u32[]{:S(2)}, u32[]{:S(2)}) collective-permute-start(f32[2,3,1,128,128]{4,3,0,2,1:T(8,128)S(1)} %get-tuple-element.84), channel_id=1, source_target_pairs={{0,1},{1,2},{2,3},{3,4},{4,5},{5,6},{6,7},{7,8},{8,9},{9,10},{10,1... | collective-permute-start | bytes 1179656 | tf_op jit(solution)/shard_map/ppermute | solution.py:23
  421.0 364.9 %all-gather.16.cloned.1.call-start = ((), (), s32[]{:S(2)}) async-start(), calls=%async_computation.3 | async-start | bytes 4325376 | tf_op jit(solution)/shard_map/all_gather | solution.py:82
  424.3 12.5 %collective-permute-start.13 = (f32[2,3,1,128,128]{4,3,0,2,1:T(8,128)S(1)}, f32[2,3,1,128,128]{4,3,0,2,1:T(8,128)S(1)}, u32[]{:S(2)}, u32[]{:S(2)}) collective-permute-start(f32[2,3,1,128,128]{4,3,0,2,1:T(8,128)S(1)} %get-tuple-element.82), channel_id=1, source_target_pairs={{0,1},{1,2},{2,3},{3,4},{4,5},{5,6},{6,7},{7,8},{8,9},{9,10},{10,1... | collective-permute-start | bytes 1179656 | tf_op jit(solution)/shard_map/ppermute | solution.py:23
  590.8 11.7 collective-permute-start.15
  608.9 13.5 %collective-permute-start.17 = (f32[2,3,1,128,128]{4,3,0,2,1:T(8,128)S(1)}, f32[2,3,1,128,128]{4,3,0,2,1:T(8,128)S(1)}, u32[]{:S(2)}, u32[]{:S(2)}) collective-permute-start(f32[2,3,1,128,128]{4,3,0,2,1:T(8,128)S(1)} %get-tuple-element.78), channel_id=1, source_target_pairs={{0,1},{1,2},{2,3},{3,4},{4,5},{5,6},{6,7},{7,8},{8,9},{9,10},{10,1... | collective-permute-start | bytes 1179656 | tf_op jit(solution)/shard_map/ppermute | solution.py:23
  635.2 12.5 %collective-permute-start.19 = (f32[2,3,1,128,128]{4,3,0,2,1:T(8,128)S(1)}, f32[2,3,1,128,128]{4,3,0,2,1:T(8,128)S(1)}, u32[]{:S(2)}, u32[]{:S(2)}) collective-permute-start(f32[2,3,1,128,128]{4,3,0,2,1:T(8,128)S(1)} %get-tuple-element.76), channel_id=1, source_target_pairs={{0,1},{1,2},{2,3},{3,4},{4,5},{5,6},{6,7},{7,8},{8,9},{9,10},{10,1... | collective-permute-start | bytes 1179656 | tf_op jit(solution)/shard_map/ppermute | solution.py:23
  802.0 11.7 collective-permute-start.21
  817.1 13.3 %collective-permute-start.22 = (f32[2,3,1,128,128]{4,3,0,2,1:T(8,128)S(1)}, f32[2,3,1,128,128]{4,3,0,2,1:T(8,128)S(1)}, u32[]{:S(2)}, u32[]{:S(2)}) collective-permute-start(f32[2,3,1,128,128]{4,3,0,2,1:T(8,128)S(1)} %get-tuple-element.73), channel_id=1, source_target_pairs={{1,0},{2,1},{3,2},{4,3},{5,4},{6,5},{7,6},{8,7},{9,8},{10,9},{11,1... | collective-permute-start | bytes 1179656 | tf_op jit(solution)/shard_map/ppermute | solution.py:25
  820.0 13.2 %collective-permute-start.23 = (f32[2,3,1,128,128]{4,3,0,2,1:T(8,128)S(1)}, f32[2,3,1,128,128]{4,3,0,2,1:T(8,128)S(1)}, u32[]{:S(2)}, u32[]{:S(2)}) collective-permute-start(f32[2,3,1,128,128]{4,3,0,2,1:T(8,128)S(1)} %get-tuple-element.72), channel_id=1, source_target_pairs={{0,1},{1,2},{2,3},{3,4},{4,5},{5,6},{6,7},{7,8},{8,9},{9,10},{10,1... | collective-permute-start | bytes 1179656 | tf_op jit(solution)/shard_map/ppermute | solution.py:23
  822.5 37.9 %collective-permute-start.31 = (f32[2,3,1,128,128]{4,3,0,2,1:T(8,128)S(1)}, f32[2,3,1,128,128]{4,3,0,2,1:T(8,128)S(1)}, u32[]{:S(2)}, u32[]{:S(2)}) collective-permute-start(f32[2,3,1,128,128]{4,3,0,2,1:T(8,128)S(1)} %get-tuple-element.68), channel_id=1, source_target_pairs={{1,0},{2,1},{3,2},{4,3},{5,4},{6,5},{7,6},{8,7},{9,8},{10,9},{11,1... | collective-permute-start | bytes 1179656 | tf_op jit(solution)/shard_map/ppermute | solution.py:25
  828.3 32.0 %collective-permute-start.32 = (f32[2,3,1,128,128]{4,3,0,2,1:T(8,128)S(1)}, f32[2,3,1,128,128]{4,3,0,2,1:T(8,128)S(1)}, u32[]{:S(2)}, u32[]{:S(2)}) collective-permute-start(f32[2,3,1,128,128]{4,3,0,2,1:T(8,128)S(1)} %get-tuple-element.67), channel_id=1, source_target_pairs={{0,1},{1,2},{2,3},{3,4},{4,5},{5,6},{6,7},{7,8},{8,9},{9,10},{10,1... | collective-permute-start | bytes 1179656 | tf_op jit(solution)/shard_map/ppermute | solution.py:23
  836.6 32.7 %collective-permute-start.24 = (f32[1,3,4,128,128]{4,3,0,2,1:T(8,128)S(1)}, f32[1,3,4,128,128]{4,3,0,2,1:T(8,128)S(1)}, u32[]{:S(2)}, u32[]{:S(2)}) collective-permute-start(f32[1,3,4,128,128]{4,3,0,2,1:T(8,128)S(1)} %slice.1534), channel_id=1, source_target_pairs={{0,32},{32,64},{64,96},{96,0},{1,33},{33,65},{65,97},{97,1},{2,34}... | collective-permute-start | bytes 2359304 | tf_op jit(solution)/shard_map/ppermute | solution.py:35
  869.3 16.0 %collective-permute-start.25 = (f32[1,3,1,128,128]{4,3,0,2,1:T(8,128)S(1)}, f32[1,3,1,128,128]{4,3,0,2,1:T(8,128)S(1)}, u32[]{:S(2)}, u32[]{:S(2)}) collective-permute-start(f32[1,3,1,128,128]{4,3,0,2,1:T(8,128)S(1)} %get-tuple-element.139), channel_id=1, source_target_pairs={{1,0},{2,1},{3,2},{4,3},{5,4},{6,5},{7,6},{8,7},{9,8},{10,9},{11,1... | collective-permute-start | bytes 589832 | tf_op jit(solution)/shard_map/ppermute | solution.py:25
  877.0 18.2 %collective-permute-start.33 = (f32[2,3,1,128,128]{4,3,0,2,1:T(8,128)S(1)}, f32[2,3,1,128,128]{4,3,0,2,1:T(8,128)S(1)}, u32[]{:S(2)}, u32[]{:S(2)}) collective-permute-start(f32[2,3,1,128,128]{4,3,0,2,1:T(8,128)S(1)} %get-tuple-element.66), channel_id=1, source_target_pairs={{1,0},{2,1},{3,2},{4,3},{5,4},{6,5},{7,6},{8,7},{9,8},{10,9},{11,1... | collective-permute-start | bytes 1179656 | tf_op jit(solution)/shard_map/ppermute | solution.py:25
  883.4 11.8 collective-permute-start.34
  957.5 14.1 %collective-permute-start.41 = (f32[1,3,4,128,128]{4,3,0,2,1:T(8,128)}, f32[1,3,4,128,128]{4,3,0,2,1:T(8,128)}, u32[]{:S(2)}, u32[]{:S(2)}) collective-permute-start(f32[1,3,4,128,128]{4,3,0,2,1:T(8,128)} %fusion.149), channel_id=1, source_target_pairs={{0,32},{32,64},{64,96},{1,33},{33,65},{65,97},{2,34},{34,66},{66,9... | collective-permute-start | bytes 2359304 | tf_op jit(solution)/shard_map/ppermute | solution.py:41
  987.7 11.1 collective-permute-start.45
  1054.1 23.6 %collective-permute-start.54 = (f32[1,3,4,128,128]{4,3,0,2,1:T(8,128)}, f32[1,3,4,128,128]{4,3,0,2,1:T(8,128)}, u32[]{:S(2)}, u32[]{:S(2)}) collective-permute-start(f32[1,3,4,128,128]{4,3,0,2,1:T(8,128)} %fusion.129), channel_id=1, source_target_pairs={{0,32},{32,64},{64,96},{1,33},{33,65},{65,97},{2,34},{34,66},{66,9... | collective-permute-start | bytes 2359304 | tf_op jit(solution)/shard_map/ppermute | solution.py:41
  1094.0 11.8 collective-permute-start.58
  1109.4 11.1 collective-permute-start.60
  1162.4 22.6 %collective-permute-start.67 = (f32[1,3,4,128,128]{4,3,0,2,1:T(8,128)}, f32[1,3,4,128,128]{4,3,0,2,1:T(8,128)}, u32[]{:S(2)}, u32[]{:S(2)}) collective-permute-start(f32[1,3,4,128,128]{4,3,0,2,1:T(8,128)} %fusion.109), channel_id=1, source_target_pairs={{0,32},{32,64},{64,96},{1,33},{33,65},{65,97},{2,34},{34,66},{66,9... | collective-permute-start | bytes 2359304 | tf_op jit(solution)/shard_map/ppermute | solution.py:41
  1201.1 11.4 collective-permute-start.71
  (78 other events, 946.1 us)
Sparse Core Ops, SparseCore 0:
  11.8 131.4 all-gather.9
  205.2 158.8 all-gather.11
  421.1 153.5 all-gather.13
  632.1 153.7 all-gather.15
where the time goes:
time: 1260 us; the launch traced here: 1240 us
  waiting for transfers between devices  698 us (55%)
  starting transfers between devices  233 us (18%)
  other arithmetic  130 us (10%)
  blocking collectives  122 us (10%)
  matrix products  23 us (2%)
  local copies, waits for them, and re-layouts  15.3 us (1%)
  between operations  15.1 us (1%)
    all_gather x4, waiting for transfers between devices, shards(): every_row = lax.all_gather(field[:, 0, 0], 'space', axis=1, tiled=True)  408 us
    ppermute x35, waiting for transfers between devices, padded_2(): lax.ppermute(tail, axis, [(i, (i + 1) % count) for i in range(ends)])  162 us
    ppermute x35, starting transfers between devices, padded_2(): lax.ppermute(head, axis, [((i + 1) % count, i) for i in range(ends)])  103 us
    ppermute x35, starting transfers between devices, padded_2(): lax.ppermute(tail, axis, [(i, (i + 1) % count) for i in range(ends)])  102 us
    ppermute x35, waiting for transfers between devices, padded_2(): lax.ppermute(head, axis, [((i + 1) % count, i) for i in range(ends)])  66 us
    all_gather x1, blocking collectives, shards(): lax.all_gather(tiles, 'space', axis=1, tiled=True)  64 us
    all_gather x1, blocking collectives, shards(): lax.all_gather(gap_row, 'space', axis=1, tiled=True)  58 us
    ppermute x3, waiting for transfers between devices, passed_along_2(): lax.ppermute(value, axis, [(source, source + steps) for source in range(f...  56.3 us
  transfers between devices with their start and end apart: 78, of which 66 were waited for; matrix products, arithmetic and copies ran while one was open for 3% of the time, Pallas kernels for 0%

commit v1 on v0

v1 whole, which is shorter than its diff:
```python
import jax
import jax.numpy as jnp
from jax import lax
from jax.experimental import pallas as pl
from jax.experimental.pallas import tpu as pltpu
from jax.sharding import PartitionSpec as P

STEPS = 4
SWEEPS = 3
CAP = 8
PAD = 8

INVERSE_STEP = 2.0
GAP_GAIN = 1.0
MESH = pl.DeviceIdType.MESH
HIGHEST = lax.Precision.HIGHEST


def kernel(
    n_space, n_tm,
    states, sources, conduct, gap_tile, gap_row,
    out,
    v, rhs, sig, alpha, dinv, w1, w2, delta, cond8, gamma, dinv_c, new0, passed,
    pick, place, packed, landed, names, names_in, coupled,
    halo_send, halo_recv, gap_send, gap_recv, name_send, name_recv,
    cond_send, cond_recv, delta_send, delta_recv, pass_send, pass_recv,
):
    me = lax.axis_index("space")
    rank = lax.axis_index("tm")
    n_slice, n_comp, planes, rows, width = states.shape
    slots = n_space * CAP
    inner = pl.ds(PAD, rows)
    left_dev = {"space": jnp.maximum(me - 1, 0)}
    right_dev = {"space": jnp.minimum(me + 1, n_space - 1)}
    has_left = me > 0
    has_right = me < n_space - 1
    lane = lax.broadcasted_iota(jnp.int32, (rows, width), 1)
    sub = lax.broadcasted_iota(jnp.int32, (rows, width), 0)

    edge_rows = jnp.zeros((PAD, width), jnp.float32)
    no_plane = jnp.zeros((rows, width), jnp.float32)

    def pad_planes(ref, index, count):
        for p in range(count):
            ref[index + (p, pl.ds(0, PAD))] = edge_rows
            ref[index + (p, pl.ds(PAD + rows, PAD))] = edge_rows

    def pad_fields(i, _):
        s, c = i // n_comp, i % n_comp
        for par in range(2):
            pad_planes(v, (par, s, c), planes + 2)
        pad_planes(delta, (s, c), planes + 6)
        for p in range(planes):
            v[0, s, c, p + 1, inner] = states[s, c, p]
        return 0

    lax.fori_loop(0, n_slice * n_comp, pad_fields, 0)
    pad_planes(w1, (), planes + 4)
    pad_planes(w2, (), planes + 2)

    def clear(first, past):
        def one(i, _):
            s, c = i // n_comp, i % n_comp
            for par in range(2):
                v[par, s, c, 0 if first else planes + 1, inner] = no_plane
            for p in range(3):
                delta[s, c, p if first else planes + 3 + p, inner] = no_plane
            return 0

        lax.fori_loop(0, n_slice * n_comp, one, 0)
        for p in range(2):
            cond8[p if first else planes + 2 + p] = no_plane

    @pl.when(jnp.logical_not(has_left))
    def _():
        clear(True, 0)

    @pl.when(jnp.logical_not(has_right))
    def _():
        clear(False, 0)

    barrier = pltpu.get_barrier_semaphore()

    def greet(i, _):
        peer = lax.rem(me + i, n_space)
        pl.semaphore_signal(barrier, inc=1, device_id={"space": peer}, device_id_type=MESH)
        return 0

    lax.fori_loop(1, n_space, greet, 0)
    next_rank = lax.rem(rank + 1, n_tm)
    for peer in (next_rank, lax.rem(rank + n_tm - 1, n_tm)):
        pl.semaphore_signal(barrier, inc=1, device_id={"tm": peer}, device_id_type=MESH)

    for p in range(planes):
        rate = INVERSE_STEP * conduct[p]
        inverse = 1.0 / (rate + 6.0)
        dinv[p] = inverse
        alpha[p] = rate * inverse
        cond8[p + 2] = conduct[p]

    def scaled(i, _):
        s, c = i // n_comp, i % n_comp
        for p in range(planes):
            sig[s, c, p] = sources[s, c, p] * dinv[p]
        return 0

    lax.fori_loop(0, n_slice * n_comp, scaled, 0)

    for s in range(n_slice):
        tile_col = jnp.broadcast_to(gap_tile[s].astype(jnp.float32), (rows, width))
        tile_row = tile_col.T
        before = jnp.where((tile_col == tile_row) & (sub < lane), 1.0, 0.0)
        position = jnp.sum(before, axis=0, keepdims=True)
        slot = tile_row[0:1] * CAP + position
        wide = lax.broadcasted_iota(jnp.int32, (slots, rows), 0).astype(jnp.float32)
        chosen = jnp.where(wide == slot, 1.0, 0.0)
        pick[s] = chosen
        target = gap_row[s:s + 1].astype(jnp.float32) + 1.0
        named = jnp.sum(chosen * target, axis=1, keepdims=True)
        names[s] = jnp.broadcast_to(named, (slots, width))

    def pack(s, gp, par):
        packed[gp, s] = jnp.dot(
            pick[s], v[par, s, 0, 1, inner], precision=HIGHEST, preferred_element_type=jnp.float32
        )

    for s in range(n_slice):
        pack(s, 0, 0)

    pl.semaphore_wait(barrier, n_space - 1 + 2)

    def halo_copy(par, s, c, way):
        return pltpu.make_async_remote_copy(
            src_ref=v.at[par, s, c, 1 if way == 0 else planes, inner],
            dst_ref=v.at[par, s, c, planes + 1 if way == 0 else 0, inner],
            send_sem=halo_send.at[par, s, c, way],
            recv_sem=halo_recv.at[par, s, c, way],
            device_id=left_dev if way == 0 else right_dev,
            device_id_type=MESH,
        )

    def delta_copy(s, c, way):
        return pltpu.make_async_remote_copy(
            src_ref=delta.at[s, c, pl.ds(3 if way == 0 else planes, 3), inner],
            dst_ref=delta.at[s, c, pl.ds(planes + 3 if way == 0 else 0, 3), inner],
            send_sem=delta_send.at[s, c, way],
            recv_sem=delta_recv.at[s, c, way],
            device_id=left_dev if way == 0 else right_dev,
            device_id_type=MESH,
        )

    def cond_copy(way):
        return pltpu.make_async_remote_copy(
            src_ref=cond8.at[pl.ds(2 if way == 0 else planes, 2)],
            dst_ref=cond8.at[pl.ds(planes + 2 if way == 0 else 0, 2)],
            send_sem=cond_send.at[way],
            recv_sem=cond_recv.at[way],
            device_id=left_dev if way == 0 else right_dev,
            device_id_type=MESH,
        )

    def start(copy):
        @pl.when(has_left)
        def _():
            copy(0).start()

        @pl.when(has_right)
        def _():
            copy(1).start()

    def arrived(copy):
        @pl.when(has_right)
        def _():
            copy(0).wait_recv()

        @pl.when(has_left)
        def _():
            copy(1).wait_recv()

    def sent(copy):
        @pl.when(has_left)
        def _():
            copy(0).wait_send()

        @pl.when(has_right)
        def _():
            copy(1).wait_send()

    def scatter(source, landing, send_sem, recv_sem):
        def one(i, _):
            peer = lax.rem(me + i, n_space)
            pltpu.make_async_remote_copy(
                src_ref=source.at[:, pl.ds(pl.multiple_of(peer * CAP, CAP), CAP)],
                dst_ref=landing.at[:, pl.ds(pl.multiple_of(me * CAP, CAP), CAP)],
                send_sem=send_sem,
                recv_sem=recv_sem,
                device_id={"space": peer},
                device_id_type=MESH,
            ).start()
            return 0

        lax.fori_loop(1, n_space, one, 0)
        own = pl.ds(pl.multiple_of(me * CAP, CAP), CAP)
        for s in range(n_slice):
            landing[s, own] = source[s, own]

    def all_of(source, landing, send_sem, recv_sem):
        most = pl.ds(0, (n_space - 1) * CAP)
        return pltpu.make_async_remote_copy(
            src_ref=source.at[:, most],
            dst_ref=landing.at[:, most],
            send_sem=send_sem,
            recv_sem=recv_sem,
            device_id=left_dev,
            device_id_type=MESH,
        )

    def gap_refs(gp):
        return packed.at[gp], landed.at[gp], gap_send.at[gp], gap_recv.at[gp]

    name_refs = (names, names_in, name_send.at[0], name_recv.at[0])
    scatter(*name_refs)
    scatter(*gap_refs(0))

    def start_all(i, _):
        s, c = i // n_comp, i % n_comp
        start(lambda way: halo_copy(0, s, c, way))
        return 0

    lax.fori_loop(0, n_slice * n_comp, start_all, 0)
    start(cond_copy)

    def beside(ref, index, p):
        here = ref[index + (p, inner)]
        total = ref[index + (p - 1, inner)] + ref[index + (p + 1, inner)]
        total = total + ref[index + (p, pl.ds(PAD - 1, rows))] + ref[index + (p, pl.ds(PAD + 1, rows))]
        total = total + jnp.where(lane == 0, 0.0, pltpu.roll(here, 1, 1))
        total = total + jnp.where(lane == width - 1, 0.0, pltpu.roll(here, width - 1, 1))
        return total, here

    def field(step, sweep, s, c, gap):
        count = step * SWEEPS + sweep
        par = lax.rem(count, 2)
        onto = 1 - par
        arrived(lambda way: halo_copy(par, s, c, way))

        @pl.when(count > 0)
        def _():
            sent(lambda way: halo_copy(onto, s, c, way))

        def plane(p):
            total, here = beside(v, (par, s, c), p)
            if sweep == 0:
                base = alpha[p - 1] * here + sig[s, c, p - 1]
                if gap and p == 1:
                    base = base + dinv[0] * coupled[s]
                rhs[s, c, p - 1] = base
            else:
                base = rhs[s, c, p - 1]
            v[onto, s, c, p, inner] = base + dinv[p - 1] * total

        plane(1)
        plane(planes)
        more = step < STEPS - 1 if sweep == SWEEPS - 1 else None

        def send():
            start(lambda way: halo_copy(onto, s, c, way))

        if more is None:
            send()
        else:
            pl.when(more)(send)
        for p in range(2, planes):
            plane(p)

    def one_step(step, _):
        gp = lax.rem(step, 2)
        for sweep in range(SWEEPS):

            def free(i, _, sweep=sweep):
                field(step, sweep, i // 2, 1 + i % 2, False)
                return 0

            lax.fori_loop(0, n_slice * 2, free, 0)
            if sweep == 0:

                @pl.when(step == 0)
                def _():
                    all_of(*name_refs).wait_recv()
                    for s in range(n_slice):
                        for part in range(2):
                            held = names_in[s, pl.ds(part * 128, 128)]
                            hit = jnp.where(held == (lane + 1).astype(jnp.float32), 1.0, 0.0)
                            place[s, :, pl.ds(part * 128, 128)] = hit.T

                all_of(*gap_refs(gp)).wait_recv()
                for s in range(n_slice):
                    coupled[s] = GAP_GAIN * jnp.dot(
                        place[s], landed[gp, s], precision=HIGHEST, preferred_element_type=jnp.float32
                    )

            def tied(s, _, sweep=sweep):
                field(step, sweep, s, 0, True)
                return 0

            lax.fori_loop(0, n_slice, tied, 0)

        @pl.when(step < STEPS - 1)
        def _():
            later = 1 - gp
            par = lax.rem((step + 1) * SWEEPS, 2)

            @pl.when(step > 0)
            def _():
                all_of(*gap_refs(later)).wait_send()

            for s in range(n_slice):
                pack(s, later, par)
            scatter(*gap_refs(later))

        return 0

    lax.fori_loop(0, STEPS, one_step, 0)
    end = (STEPS * SWEEPS) % 2

    def pass_copy(source, c):
        return pltpu.make_async_remote_copy(
            src_ref=source,
            dst_ref=new0.at[c],
            send_sem=pass_send.at[c],
            recv_sem=pass_recv.at[c],
            device_id={"tm": next_rank},
            device_id_type=MESH,
        )

    @pl.when(rank == n_tm - 1)
    def _():
        def one(c, _):
            pass_copy(v.at[end, n_slice - 1, c, pl.ds(1, planes), inner], c).start()
            return 0

        lax.fori_loop(0, n_comp, one, 0)

    arrived(cond_copy)
    for p in range(planes + 4):
        rate = INVERSE_STEP * cond8[p] / STEPS
        inverse = 1.0 / (rate + 6.0)
        if p < 2:
            inverse = jnp.where(has_left, inverse, 0.0)
        if p >= planes + 2:
            inverse = jnp.where(has_right, inverse, 0.0)
        dinv_c[p] = inverse
        gamma[p] = rate * inverse

    def coarse(s, c, p):
        total, _ = beside(w2, (), p + 1)
        return gamma[p + 2] * delta[s, c, p + 3, inner] + dinv_c[p + 2] * total

    def coarse_before(s, c):
        for p in range(planes + 4):
            total, here = beside(delta, (s, c), p + 1)
            w1[p, inner] = gamma[p] * here + dinv_c[p] * total
        for p in range(planes + 2):
            total, _ = beside(w1, (), p + 1)
            w2[p, inner] = gamma[p + 1] * delta[s, c, p + 2, inner] + dinv_c[p + 1] * total

    def first(c, _):
        pass_copy(new0.at[c], c).wait_recv()
        for p in range(planes):
            value = new0[c, p]
            out[0, c, p] = value
            delta[0, c, p + 3, inner] = value - states[0, c, p]
        start(lambda way: delta_copy(0, c, way))
        return 0

    lax.fori_loop(0, n_comp, first, 0)

    def second(c, _):
        arrived(lambda way: delta_copy(0, c, way))
        coarse_before(0, c)
        for p in range(planes):
            value = coarse(0, c, p) + v[end, 0, c, p + 1, inner]
            out[1, c, p] = value
            delta[1, c, p + 3, inner] = value - states[1, c, p]

        @pl.when(rank < n_tm - 1)
        def _():
            start(lambda way: delta_copy(1, c, way))

        return 0

    lax.fori_loop(0, n_comp, second, 0)

    @pl.when(rank < n_tm - 1)
    def _():
        def third(c, _):
            arrived(lambda way: delta_copy(1, c, way))
            coarse_before(1, c)
            for p in range(planes):
                passed[c, p] = coarse(1, c, p) + v[end, 1, c, p + 1, inner]
            pass_copy(passed.at[c], c).start()
            return 0

        lax.fori_loop(0, n_comp, third, 0)

    def leave(i, _):
        s, c = i // n_comp, i % n_comp
        sent(lambda way: halo_copy(1 - end, s, c, way))
        return 0

    lax.fori_loop(0, n_slice * n_comp, leave, 0)
    sent(cond_copy)
    all_of(*name_refs).wait_send()
    for gp in range(2):
        all_of(*gap_refs(gp)).wait_send()
    for c in range(n_comp):
        sent(lambda way: delta_copy(0, c, way))
        pass_copy(passed.at[c], c).wait_send()

        @pl.when(rank < n_tm - 1)
        def _():
            sent(lambda way: delta_copy(1, c, way))


def solution(mesh):
    n_space, n_tm = mesh.shape["space"], mesh.shape["tm"]

    def shards(states, sources, conductivity, gap_tile, gap_row):
        n_slice, n_comp, planes, rows, width = states.shape
        high = rows + 2 * PAD
        slots = n_space * CAP

        def f32(*shape):
            return pltpu.VMEM(shape, jnp.float32)

        def dma(*shape):
            return pltpu.SemaphoreType.DMA(shape)

        def body(*refs):
            kernel(n_space, n_tm, *refs)

        vmem = pl.BlockSpec(memory_space=pltpu.VMEM)
        return pl.pallas_call(
            body,
            out_shape=jax.ShapeDtypeStruct(states.shape, jnp.float32),
            in_specs=[vmem] * 5,
            out_specs=vmem,
            scratch_shapes=[
                f32(2, n_slice, n_comp, planes + 2, high, width),
                f32(n_slice, n_comp, planes, rows, width),
                f32(n_slice, n_comp, planes, rows, width),
                f32(planes, rows, width),
                f32(planes, rows, width),
                f32(planes + 4, high, width),
                f32(planes + 2, high, width),
                f32(n_slice, n_comp, planes + 6, high, width),
                f32(planes + 4, rows, width),
                f32(planes + 4, rows, width),
                f32(planes + 4, rows, width),
                f32(n_comp, planes, rows, width),
                f32(n_comp, planes, rows, width),
                f32(n_slice, slots, rows),
                f32(n_slice, rows, slots),
                f32(2, n_slice, slots, width),
                f32(2, n_slice, slots, width),
                f32(n_slice, slots, width),
                f32(n_slice, slots, width),
                f32(n_slice, rows, width),
                dma(2, n_slice, n_comp, 2), dma(2, n_slice, n_comp, 2),
                dma(2), dma(2), dma(1), dma(1), dma(2), dma(2),
                dma(n_slice, n_comp, 2), dma(n_slice, n_comp, 2), dma(n_comp), dma(n_comp),
            ],
            compiler_params=pltpu.CompilerParams(
                collective_id=0, has_side_effects=True, vmem_limit_bytes=48 * 1024 * 1024
            ),
        )(states, sources, conductivity, gap_tile, gap_row)

    return jax.shard_map(
        shards,
        mesh=mesh,
        in_specs=(
            P("tm", None, "space", None, None),
            P("tm", None, "space", None, None),
            P("space", None, None),
            P("tm", "space", None),
            P("tm", "space"),
        ),
        out_specs=P("tm", None, "space", None, None),
        check_vma=False,
    )
```

time: 1260 us -> 214 us (0.17); the launches traced: 1240 us -> 214 us
  waiting for transfers between devices: 698 us -> 0 us
  starting transfers between devices: 233 us -> 0 us
  Pallas kernels: 0 us -> 207 us
  other arithmetic: 130 us -> 0 us
  blocking collectives: 122 us -> 0 us
  matrix products: 23 us -> 0 us
  between operations: 15.1 us -> 0.03 us
    all_gather x4 -> x0, waiting for transfers between devices: 408 us -> none  [shards(): every_row = lax.all_gather(field[:, 0, 0], 'space', axis=1, tiled=True)]
    ppermute x74 -> x0, waiting for transfers between devices: 290 us -> none  [the longest x35 162 us: padded_2(): lax.ppermute(tail, axis, [(i, (i + 1) % count) for i in range(ends)])]
    ppermute x74 -> x0, starting transfers between devices: 233 us -> none  [the longest x35 103 us: padded_2(): lax.ppermute(head, axis, [((i + 1) % count, i) for i in range(ends)])]
    pallas_call x0 -> x1, Pallas kernels: none -> 207 us  [shards(): pl.pallas_call(body, out_shape=jax.ShapeDtypeStruct(states.shape, jnp.flo...]
    all_gather x2 -> x0, blocking collectives: 122 us -> none  [the longest x1 64 us: shards(): lax.all_gather(tiles, 'space', axis=1, tiled=True)]
    concatenate x36 -> x0, other arithmetic: 54.1 us -> none  [the longest x35 54 us: padded_2(): jnp.concatenate([lax.ppermute(tail, axis, [(i, (i + 1) % count) for i in...]
    div x27 -> x0, other arithmetic: 51.2 us -> none  [the longest x26 50.2 us: jacobi(): field = (rhs + neighbours(field)) / diag]
    dot_general x4 -> x0, matrix products: 23 us -> none  [shards(): jnp.einsum('syr,srz->syz', mine, every_row, precision=lax.Precision.HIGHEST)]
  transfers between devices with their start and end apart: 78 -> 0, of which waited for: 66 -> 0; matrix products, arithmetic and copies ran while one was open for 3% -> 0% of each run, Pallas kernels for 0% -> 0%
where the time goes in v1:
time: 214 us
  Pallas kernels  207 us (97%)
  local copies, waits for them, and re-layouts  6.39 us (3%)
    pallas_call x1, Pallas kernels, shards(): pl.pallas_call(body, out_shape=jax.ShapeDtypeStruct(states.shape, jnp.flo...  207 us
    unnamed x10, local copies, waits for them, and re-layouts  6.39 us

profile of v1, /device:TPU:13, one launch (start us, length us, event | category | flops | bytes accessed | tf_op | source)
XLA Modules:
  0.0 213.6 jit_solution(10492749390429556643)
XLA Ops:
  0.0 0.8 copy.6.refs_3_
  0.8 0.0 copy-start
  0.8 1.4 copy-done
  2.2 0.0 copy-start.1
  2.2 1.4 copy-done.1
  3.6 0.0 copy-start.2
  3.6 0.9 copy-done.2
  4.6 0.0 copy-start.3
  4.6 0.7 copy-done.3
  5.3 207.2 %shard_map.55 = f32[2,3,4,128,128]{4,3,2,1,0:T(8,128)S(1)} custom-call(f32[2,3,4,128,128]{4,3,2,1,0:T(8,128)S(1)} %copy-done, f32[2,3,4,128,128]{4,3,2,1,0:T(8,128)S(1)} %copy-done.1, f32[4,128,128]{2,1,0:T(8,128)S(1)} %copy-done.2, s32[2,128,1]{2,1,0:T(8,128)S(1)} %copy.6.refs_3_, s32[2,128]{1,0:T(2,128)S(1)} %copy-done.3), custom_call_target="tpu_custom_call" | custom-call | tf_op jit(solution)/shard_map/pallas_call | solution.py:443
  212.5 1.1 copy.8
Async XLA Ops:
  0.8 1.4 copy-start
  2.2 1.4 copy-start.1
  3.6 0.9 copy-start.2
  4.6 0.7 copy-start.3

commit v2 on v1

v2 whole, which is shorter than its diff:
```python
import jax
import jax.numpy as jnp
from jax import lax
from jax.experimental import pallas as pl
from jax.experimental.pallas import tpu as pltpu
from jax.sharding import PartitionSpec as P

STEPS = 4
SWEEPS = 3
CAP = 8
PAD = 8

FREE = ((0, 6), (6, 9), (9, 12))
OPENING = (0, 1, 2, 3, 4, 5)
EARLY = 2
LAG = 2

INVERSE_STEP = 2.0
GAP_GAIN = 1.0
MESH = pl.DeviceIdType.MESH
HIGHEST = lax.Precision.HIGHEST


def kernel(
    n_space, n_tm,
    states, sources, conduct, gap_tile, gap_row,
    out,
    v, rhs, sig, alpha, dinv, w1, w2, delta, cond8, gamma, dinv_c, start_state, new0, passed,
    tile_in, row_in, pick, place, opening, opening_in, packed, landed, coupled,
    load_sem, halo_send, halo_recv, gap_send, gap_recv,
    cond_send, cond_recv, delta_send, delta_recv, pass_send, pass_recv, turn,
):
    me = lax.axis_index("space")
    rank = lax.axis_index("tm")
    n_slice, n_comp, planes, rows, width = states.shape
    slots = n_space * CAP
    inner = pl.ds(PAD, rows)
    left_dev = {"space": jnp.maximum(me - 1, 0)}
    right_dev = {"space": jnp.minimum(me + 1, n_space - 1)}
    has_left = me > 0
    has_right = me < n_space - 1
    lane = lax.broadcasted_iota(jnp.int32, (rows, width), 1)
    sub = lax.broadcasted_iota(jnp.int32, (rows, width), 0)

    n_field = n_slice * n_comp
    n_free = n_field - n_slice

    def place_of(s, c):
        return jnp.where(c == 0, n_free + s, s * (n_comp - 1) + c - 1)

    barrier = pltpu.get_barrier_semaphore()

    def greet(i, _):
        peer = lax.rem(me + i, n_space)
        pl.semaphore_signal(barrier, inc=1, device_id={"space": peer}, device_id_type=MESH)
        return 0

    lax.fori_loop(1, n_space, greet, 0)
    next_rank = lax.rem(rank + 1, n_tm)
    for peer in (next_rank, lax.rem(rank + n_tm - 1, n_tm)):
        pl.semaphore_signal(barrier, inc=1, device_id={"tm": peer}, device_id_type=MESH)

    fields = [(s, c) for s in range(n_slice) for c in range(n_comp)]
    slot_of = {(s, c): n_free + s if c == 0 else s * (n_comp - 1) + c - 1 for s, c in fields}
    tile_load = pltpu.make_async_copy(gap_tile, tile_in, load_sem.at[0])
    row_load = pltpu.make_async_copy(gap_row, row_in, load_sem.at[1])
    cond_load = pltpu.make_async_copy(conduct, cond8.at[pl.ds(2, planes)], load_sem.at[2])
    state_load = pltpu.make_async_copy(states, start_state, load_sem.at[3])
    field_loads = {
        (s, c): pltpu.make_async_copy(
            states.at[s, c], v.at[0, slot_of[s, c], pl.ds(1, planes), inner], load_sem.at[4 + slot_of[s, c]]
        )
        for s, c in fields
    }
    source_loads = {
        (s, c): pltpu.make_async_copy(
            sources.at[s, c], sig.at[slot_of[s, c]], load_sem.at[4 + n_field + slot_of[s, c]]
        )
        for s, c in fields
    }
    tile_load.start()
    row_load.start()
    cond_load.start()
    for at in sorted(fields, key=lambda at: at[1]):
        field_loads[at].start()
    for at in fields:
        source_loads[at].start()
    state_load.start()

    edge_rows = jnp.zeros((PAD, width), jnp.float32)
    no_plane = jnp.zeros((rows, width), jnp.float32)

    def pad_planes(ref, index, count):
        for p in range(count):
            ref[index + (p, pl.ds(0, PAD))] = edge_rows
            ref[index + (p, pl.ds(PAD + rows, PAD))] = edge_rows

    def pad_fields(i, _):
        s, c = i // n_comp, i % n_comp
        f = place_of(s, c)
        for par in range(2):
            pad_planes(v, (par, f), planes + 2)
        pad_planes(delta, (s, c), planes + 6)
        return 0

    lax.fori_loop(0, n_slice * n_comp, pad_fields, 0)
    pad_planes(w1, (), planes + 4)
    pad_planes(w2, (), planes + 2)

    def clear(first, past):
        def one(i, _):
            s, c = i // n_comp, i % n_comp
            for par in range(2):
                v[par, i, 0 if first else planes + 1, inner] = no_plane
            for p in range(3):
                delta[s, c, p if first else planes + 3 + p, inner] = no_plane
            return 0

        lax.fori_loop(0, n_slice * n_comp, one, 0)
        for p in range(2):
            cond8[p if first else planes + 2 + p] = no_plane

    @pl.when(jnp.logical_not(has_left))
    def _():
        clear(True, 0)

    @pl.when(jnp.logical_not(has_right))
    def _():
        clear(False, 0)

    tile_load.wait()
    row_load.wait()
    for s in range(n_slice):
        tile_row = jnp.broadcast_to(tile_in[s:s + 1].astype(jnp.float32), (rows, width))
        tile_col = tile_row.T
        before = jnp.where((tile_col == tile_row) & (sub < lane), 1.0, 0.0)
        position = jnp.sum(before, axis=0, keepdims=True)
        slot = tile_row[0:1] * CAP + position
        wide = lax.broadcasted_iota(jnp.int32, (slots, rows), 0).astype(jnp.float32)
        chosen = jnp.where(wide == slot, 1.0, 0.0)
        pick[s] = chosen
        target = row_in[s:s + 1].astype(jnp.float32) + 1.0
        named = jnp.sum(chosen * target, axis=1, keepdims=True)
        opening[n_slice + s] = jnp.broadcast_to(named, (slots, width))

    def packed_rows(s, par):
        return jnp.dot(
            pick[s], v[par, n_free + s, 1, inner], precision=HIGHEST, preferred_element_type=jnp.float32
        )

    for at in fields:
        field_loads[at].wait()
    for s in range(n_slice):
        opening[s] = packed_rows(s, 0)

    def fine_coefficients():
        for p in range(planes):
            rate = INVERSE_STEP * cond8[p + 2]
            inverse = 1.0 / (rate + 6.0)
            dinv[p] = inverse
            alpha[p] = rate * inverse
        for at in fields:
            source_loads[at].wait()

        def scaled(f, _):
            for p in range(planes):
                sig[f, p] = sig[f, p] * dinv[p]
            return 0

        lax.fori_loop(0, n_field, scaled, 0)

    cond_load.wait()
    pl.semaphore_wait(barrier, n_space - 1 + 2)

    def halo_copy(par, f, way):
        return pltpu.make_async_remote_copy(
            src_ref=v.at[par, f, 1 if way == 0 else planes, inner],
            dst_ref=v.at[par, f, planes + 1 if way == 0 else 0, inner],
            send_sem=halo_send.at[par, f, way],
            recv_sem=halo_recv.at[par, f, way],
            device_id=left_dev if way == 0 else right_dev,
            device_id_type=MESH,
        )

    def delta_copy(s, c, way):
        return pltpu.make_async_remote_copy(
            src_ref=delta.at[s, c, pl.ds(3 if way == 0 else planes, 3), inner],
            dst_ref=delta.at[s, c, pl.ds(planes + 3 if way == 0 else 0, 3), inner],
            send_sem=delta_send.at[s, c, way],
            recv_sem=delta_recv.at[s, c, way],
            device_id=left_dev if way == 0 else right_dev,
            device_id_type=MESH,
        )

    def cond_copy(way):
        return pltpu.make_async_remote_copy(
            src_ref=cond8.at[pl.ds(2 if way == 0 else planes, 2)],
            dst_ref=cond8.at[pl.ds(planes + 2 if way == 0 else 0, 2)],
            send_sem=cond_send.at[way],
            recv_sem=cond_recv.at[way],
            device_id=left_dev if way == 0 else right_dev,
            device_id_type=MESH,
        )

    def start(copy):
        @pl.when(has_left)
        def _():
            copy(0).start()

        @pl.when(has_right)
        def _():
            copy(1).start()

    def arrived(copy):
        @pl.when(has_right)
        def _():
            copy(0).wait_recv()

        @pl.when(has_left)
        def _():
            copy(1).wait_recv()

    def sent(copy):
        @pl.when(has_left)
        def _():
            copy(0).wait_send()

        @pl.when(has_right)
        def _():
            copy(1).wait_send()

    def scatter(source, landing, send_sem, recv_sem):
        def one(i, _):
            peer = lax.rem(me + i, n_space)
            pltpu.make_async_remote_copy(
                src_ref=source.at[:, pl.ds(pl.multiple_of(peer * CAP, CAP), CAP)],
                dst_ref=landing.at[:, pl.ds(pl.multiple_of(me * CAP, CAP), CAP)],
                send_sem=send_sem,
                recv_sem=recv_sem,
                device_id={"space": peer},
                device_id_type=MESH,
            ).start()
            return 0

        lax.fori_loop(1, n_space, one, 0)
        own = pl.ds(pl.multiple_of(me * CAP, CAP), CAP)
        for s in range(source.shape[0]):
            landing[s, own] = source[s, own]

    def all_of(source, landing, send_sem, recv_sem):
        most = pl.ds(0, (n_space - 1) * CAP)
        return pltpu.make_async_remote_copy(
            src_ref=source.at[:, most],
            dst_ref=landing.at[:, most],
            send_sem=send_sem,
            recv_sem=recv_sem,
            device_id=left_dev,
            device_id_type=MESH,
        )

    def gap_refs(gp):
        return packed.at[gp], landed.at[gp], gap_send.at[gp], gap_recv.at[gp]

    for f in OPENING:
        start(lambda way: halo_copy(0, f, way))
    opening_refs = (opening, opening_in, gap_send.at[2], gap_recv.at[2])
    scatter(*opening_refs)
    start(cond_copy)
    fine_coefficients()

    def beside(ref, index, p):
        here = ref[index + (p, inner)]
        total = ref[index + (p - 1, inner)] + ref[index + (p + 1, inner)]
        total = total + ref[index + (p, pl.ds(PAD - 1, rows))] + ref[index + (p, pl.ds(PAD + 1, rows))]
        total = total + jnp.where(lane == 0, 0.0, pltpu.roll(here, 1, 1))
        total = total + jnp.where(lane == width - 1, 0.0, pltpu.roll(here, width - 1, 1))
        return total, here

    def task(step, sweep, f, tied):
        count = step * SWEEPS + sweep
        par = lax.rem(count, 2)
        onto = 1 - par

        @pl.when(sweep == 0)
        def _():
            for p in range(planes):
                base = alpha[p] * v[par, f, p + 1, inner] + sig[f, p]
                if tied and p == 0:
                    base = base + dinv[0] * coupled[f - n_free]
                rhs[f, p] = base

        arrived(lambda way: halo_copy(par, f, way))

        @pl.when(count > 0)
        def _():
            sent(lambda way: halo_copy(onto, f, way))

        def plane(p):
            total, _ = beside(v, (par, f), p)
            v[onto, f, p, inner] = rhs[f, p - 1] + dinv[p - 1] * total

        plane(1)
        plane(planes)

        @pl.when((step < STEPS - 1) | (sweep < SWEEPS - 1))
        def _():
            start(lambda way: halo_copy(onto, f, way))

        for p in range(2, planes):
            plane(p)

    def coarse_coefficients():
        arrived(cond_copy)
        for p in range(planes + 4):
            rate = INVERSE_STEP * cond8[p] / STEPS
            inverse = 1.0 / (rate + 6.0)
            if p < 2:
                inverse = jnp.where(has_left, inverse, 0.0)
            if p >= planes + 2:
                inverse = jnp.where(has_right, inverse, 0.0)
            dinv_c[p] = inverse
            gamma[p] = rate * inverse

    state_load.wait()

    def pass_copy(source, c):
        return pltpu.make_async_remote_copy(
            src_ref=source,
            dst_ref=new0.at[c],
            send_sem=pass_send.at[c],
            recv_sem=pass_recv.at[c],
            device_id={"tm": next_rank},
            device_id_type=MESH,
        )

    def first(c, _):
        pass_copy(new0.at[c], c).wait_recv()
        for p in range(planes):
            value = new0[c, p]
            out[0, c, p] = value
            delta[0, c, p + 3, inner] = value - start_state[0, c, p]
        start(lambda way: delta_copy(0, c, way))
        return 0

    def couple(landing):
        for s in range(n_slice):
            coupled[s] = GAP_GAIN * jnp.dot(
                place[s], landing[s], precision=HIGHEST, preferred_element_type=jnp.float32
            )

    ahead = rank == n_tm - 1
    behind = rank == n_tm - 2
    beside_rank = lax.rem(rank + n_tm - 1, n_tm)

    def keep_pace(count):
        @pl.when(ahead & (count > 0) & (lax.rem(count, LAG) == 0))
        def _():
            pl.semaphore_signal(turn, inc=1, device_id={"tm": beside_rank}, device_id_type=MESH)

        @pl.when(behind & (count > 0) & (count <= STEPS * SWEEPS // LAG))
        def _():
            pl.semaphore_wait(turn, 1)

    def one_step(step, _):
        gp = lax.rem(step, 2)

        for sweep in range(SWEEPS):
            keep_pace(step * SWEEPS + sweep)

            def free(n, _):
                task(step, n // 4, n % 4, False)
                return 0

            lax.fori_loop(*FREE[sweep], free, 0)
            if sweep == 0:

                @pl.when(step == 0)
                def _():
                    all_of(*opening_refs).wait_recv()
                    for s in range(n_slice):
                        for part in range(slots // width):
                            held = opening_in[n_slice + s, pl.ds(part * width, width)]
                            hit = jnp.where(held == (lane + 1).astype(jnp.float32), 1.0, 0.0)
                            place[s, :, pl.ds(part * width, width)] = hit.T
                    couple(opening_in)

                @pl.when(step > 0)
                def _():
                    all_of(*gap_refs(gp)).wait_recv()
                    couple(landed.at[gp])

            if sweep == EARLY:
                @pl.when((rank == 0) & (step == STEPS - 1))
                def _():
                    lax.fori_loop(0, n_comp, first, 0)

            def tied(s, _, sweep=sweep):
                task(step, sweep, n_free + s, True)
                return 0

            lax.fori_loop(0, n_slice, tied, 0)

        @pl.when(step < STEPS - 1)
        def _():
            later = 1 - gp

            @pl.when(step > 1)
            def _():
                all_of(*gap_refs(later)).wait_send()

            for s in range(n_slice):
                packed[later, s] = packed_rows(s, lax.rem((step + 1) * SWEEPS, 2))
            scatter(*gap_refs(later))

        @pl.when(step == 0)
        def _():
            coarse_coefficients()

        return 0

    lax.fori_loop(0, STEPS, one_step, 0)
    keep_pace(jnp.int32(STEPS * SWEEPS))
    end = (STEPS * SWEEPS) % 2

    @pl.when(rank == n_tm - 1)
    def _():
        def one(c, _):
            pass_copy(v.at[end, place_of(n_slice - 1, c), pl.ds(1, planes), inner], c).start()
            return 0

        lax.fori_loop(0, n_comp, one, 0)

    def coarse(s, c, p):
        total, _ = beside(w2, (), p + 1)
        return gamma[p + 2] * delta[s, c, p + 3, inner] + dinv_c[p + 2] * total

    def coarse_before(s, c):
        for p in range(planes + 4):
            total, here = beside(delta, (s, c), p + 1)
            w1[p, inner] = gamma[p] * here + dinv_c[p] * total
        for p in range(planes + 2):
            total, _ = beside(w1, (), p + 1)
            w2[p, inner] = gamma[p + 1] * delta[s, c, p + 2, inner] + dinv_c[p + 1] * total

    @pl.when(rank > 0)
    def _():
        lax.fori_loop(0, n_comp, first, 0)

    def second(c, _):
        arrived(lambda way: delta_copy(0, c, way))
        coarse_before(0, c)
        for p in range(planes):
            value = coarse(0, c, p) + v[end, place_of(0, c), p + 1, inner]
            out[1, c, p] = value
            delta[1, c, p + 3, inner] = value - start_state[1, c, p]

        @pl.when(rank < n_tm - 1)
        def _():
            start(lambda way: delta_copy(1, c, way))

        return 0

    lax.fori_loop(0, n_comp, second, 0)

    @pl.when(rank < n_tm - 1)
    def _():
        def third(c, _):
            arrived(lambda way: delta_copy(1, c, way))
            coarse_before(1, c)
            for p in range(planes):
                passed[c, p] = coarse(1, c, p) + v[end, place_of(1, c), p + 1, inner]
            pass_copy(passed.at[c], c).start()
            return 0

        lax.fori_loop(0, n_comp, third, 0)

    for f in range(n_field):
        sent(lambda way: halo_copy(1 - end, f, way))
    sent(cond_copy)
    all_of(*opening_refs).wait_send()
    for gp in range(2):
        all_of(*gap_refs(gp)).wait_send()
    for c in range(n_comp):
        sent(lambda way: delta_copy(0, c, way))
        pass_copy(passed.at[c], c).wait_send()

        @pl.when(rank < n_tm - 1)
        def _():
            sent(lambda way: delta_copy(1, c, way))


def solution(mesh):
    n_space, n_tm = mesh.shape["space"], mesh.shape["tm"]

    def shards(states, sources, conductivity, gap_tile, gap_row):
        n_slice, n_comp, planes, rows, width = states.shape
        high = rows + 2 * PAD
        slots = n_space * CAP

        def f32(*shape):
            return pltpu.VMEM(shape, jnp.float32)

        def dma(*shape):
            return pltpu.SemaphoreType.DMA(shape)

        def body(*refs):
            kernel(n_space, n_tm, *refs)

        vmem = pl.BlockSpec(memory_space=pltpu.VMEM)
        return pl.pallas_call(
            body,
            out_shape=jax.ShapeDtypeStruct(states.shape, jnp.float32),
            in_specs=[pl.BlockSpec(memory_space=pl.ANY)] * 5,
            out_specs=vmem,
            scratch_shapes=[
                f32(2, n_slice * n_comp, planes + 2, high, width),
                f32(n_slice * n_comp, planes, rows, width),
                f32(n_slice * n_comp, planes, rows, width),
                f32(planes, rows, width),
                f32(planes, rows, width),
                f32(planes + 4, high, width),
                f32(planes + 2, high, width),
                f32(n_slice, n_comp, planes + 6, high, width),
                f32(planes + 4, rows, width),
                f32(planes + 4, rows, width),
                f32(planes + 4, rows, width),
                f32(n_slice, n_comp, planes, rows, width),
                f32(n_comp, planes, rows, width),
                f32(n_comp, planes, rows, width),
                pltpu.VMEM((n_slice, rows), jnp.int32),
                pltpu.VMEM((n_slice, rows), jnp.int32),
                f32(n_slice, slots, rows),
                f32(n_slice, rows, slots),
                f32(2 * n_slice, slots, width),
                f32(2 * n_slice, slots, width),
                f32(2, n_slice, slots, width),
                f32(2, n_slice, slots, width),
                f32(n_slice, rows, width),
                dma(4 + 2 * n_slice * n_comp), dma(2, n_slice * n_comp, 2), dma(2, n_slice * n_comp, 2),
                dma(3), dma(3), dma(2), dma(2),
                dma(n_slice, n_comp, 2), dma(n_slice, n_comp, 2), dma(n_comp), dma(n_comp),
                pltpu.SemaphoreType.REGULAR,
            ],
            compiler_params=pltpu.CompilerParams(
                collective_id=0, has_side_effects=True, vmem_limit_bytes=56 * 1024 * 1024
            ),
        )(states, sources, conductivity, gap_tile[:, :, 0], gap_row)

    return jax.shard_map(
        shards,
        mesh=mesh,
        in_specs=(
            P("tm", None, "space", None, None),
            P("tm", None, "space", None, None),
            P("space", None, None),
            P("tm", "space", None),
            P("tm", "space"),
        ),
        out_specs=P("tm", None, "space", None, None),
        check_vma=False,
    )
```

time: 214 us -> 204 us (0.953)
  Pallas kernels: 207 us -> 202 us
  local copies, waits for them, and re-layouts: 6.39 us -> 2.7 us
    pallas_call x1, Pallas kernels: 207 us -> 202 us  [shards(): pl.pallas_call(body, out_shape=jax.ShapeDtypeStruct(states.shape, jnp.flo...]
    unnamed x10 -> x1, local copies, waits for them, and re-layouts: 6.39 us -> 2.7 us
where the time goes in v2:
time: 204 us
  Pallas kernels  202 us (99%)
  local copies, waits for them, and re-layouts  2.7 us (1%)
    pallas_call x1, Pallas kernels, shards(): pl.pallas_call(body, out_shape=jax.ShapeDtypeStruct(states.shape, jnp.flo...  202 us

profile of v2, /device:TPU:13, one launch (start us, length us, event | category | flops | bytes accessed | tf_op | source)
XLA Modules:
  0.0 204.2 jit_solution(758208210186089291)
XLA Ops:
  0.0 201.5 %shard_map.55 = f32[2,3,4,128,128]{4,3,2,1,0:T(8,128)} custom-call(f32[2,3,4,128,128]{4,3,2,1,0:T(8,128)} %refs_0_.1, f32[2,3,4,128,128]{4,3,2,1,0:T(8,128)} %refs_1_.1, f32[4,128,128]{2,1,0:T(8,128)} %refs_2_.1, s32[2,128]{1,0:T(2,128)} %bitcast.1, s32[2,128]{1,0:T(2,128)} %refs_4_.1), custom_call_target="tpu_custom_call" | custom-call | tf_op jit(solution)/shard_map/pallas_call | solution.py:510
  201.5 2.7 %copy.7 = f32[2,3,4,128,128]{4,3,2,1,0:T(8,128)} copy(f32[2,3,4,128,128]{4,3,2,1,0:T(8,128)} %shard_map.55) | data formatting | bytes 3145728

commit v3 on v2

--- a/solution.py
+++ b/solution.py
@@ -13,7 +13,7 @@
 FREE = ((0, 6), (6, 9), (9, 12))
 OPENING = (0, 1, 2, 3, 4, 5)
 EARLY = 2
-LAG = 2
+LEADS = (1, 4)
 
 INVERSE_STEP = 2.0
 GAP_GAIN = 1.0
@@ -130,6 +130,7 @@
 
     tile_load.wait()
     row_load.wait()
+    names = []
     for s in range(n_slice):
         tile_row = jnp.broadcast_to(tile_in[s:s + 1].astype(jnp.float32), (rows, width))
         tile_col = tile_row.T
@@ -141,7 +142,9 @@
         pick[s] = chosen
         target = row_in[s:s + 1].astype(jnp.float32) + 1.0
         named = jnp.sum(chosen * target, axis=1, keepdims=True)
-        opening[n_slice + s] = jnp.broadcast_to(named, (slots, width))
+        names.append(jnp.broadcast_to(named, (slots, width)))
+    half = width // n_slice
+    opening[n_slice] = jnp.where(lax.broadcasted_iota(jnp.int32, (slots, width), 1) < half, *names)
 
     def packed_rows(s, par):
         return jnp.dot(
@@ -348,18 +351,18 @@
                 place[s], landing[s], precision=HIGHEST, preferred_element_type=jnp.float32
             )
 
-    ahead = rank == n_tm - 1
-    behind = rank == n_tm - 2
-    beside_rank = lax.rem(rank + n_tm - 1, n_tm)
+    leads = ((0, 1, LEADS[0]), (n_tm - 1, n_tm - 2, LEADS[1]))
 
     def keep_pace(count):
-        @pl.when(ahead & (count > 0) & (lax.rem(count, LAG) == 0))
-        def _():
-            pl.semaphore_signal(turn, inc=1, device_id={"tm": beside_rank}, device_id_type=MESH)
-
-        @pl.when(behind & (count > 0) & (count <= STEPS * SWEEPS // LAG))
-        def _():
-            pl.semaphore_wait(turn, 1)
+        for leader, follower, lead in leads:
+
+            @pl.when((rank == leader) & (count >= lead) & (count < STEPS * SWEEPS))
+            def _():
+                pl.semaphore_signal(turn, inc=1, device_id={"tm": follower}, device_id_type=MESH)
+
+            @pl.when((rank == follower) & (count + lead < STEPS * SWEEPS))
+            def _():
+                pl.semaphore_wait(turn, 1)
 
     def one_step(step, _):
         gp = lax.rem(step, 2)
@@ -379,7 +382,8 @@
                     all_of(*opening_refs).wait_recv()
                     for s in range(n_slice):
                         for part in range(slots // width):
-                            held = opening_in[n_slice + s, pl.ds(part * width, width)]
+                            held = opening_in[n_slice, pl.ds(part * width, width)]
+                            held = jnp.broadcast_to(held[:, s * half:s * half + 1], (width, width))
                             hit = jnp.where(held == (lane + 1).astype(jnp.float32), 1.0, 0.0)
                             place[s, :, pl.ds(part * width, width)] = hit.T
                     couple(opening_in)
@@ -419,7 +423,6 @@
         return 0
 
     lax.fori_loop(0, STEPS, one_step, 0)
-    keep_pace(jnp.int32(STEPS * SWEEPS))
     end = (STEPS * SWEEPS) % 2
 
     @pl.when(rank == n_tm - 1)
@@ -531,8 +534,8 @@
                 pltpu.VMEM((n_slice, rows), jnp.int32),
                 f32(n_slice, slots, rows),
                 f32(n_slice, rows, slots),
-                f32(2 * n_slice, slots, width),
-                f32(2 * n_slice, slots, width),
+                f32(n_slice + 1, slots, width),
+                f32(n_slice + 1, slots, width),
                 f32(2, n_slice, slots, width),
                 f32(2, n_slice, slots, width),
                 f32(n_slice, rows, width),

time: 204 us -> 199 us (0.975)
  Pallas kernels: 202 us -> 195 us
    pallas_call x1, Pallas kernels: 202 us -> 195 us  [shards(): pl.pallas_call(body, out_shape=jax.ShapeDtypeStruct(states.shape, jnp.flo...]
where the time goes in v3:
time: 199 us; the launch traced here: 197 us
  Pallas kernels  195 us (98%)
  local copies, waits for them, and re-layouts  2.7 us (1%)
    pallas_call x1, Pallas kernels, shards(): pl.pallas_call(body, out_shape=jax.ShapeDtypeStruct(states.shape, jnp.flo...  195 us

profile of v3, /device:TPU:13, one launch (start us, length us, event | category | flops | bytes accessed | tf_op | source)
XLA Modules:
  0.0 197.4 jit_solution(7511246347245166776)
XLA Ops:
  0.0 194.7 %shard_map.55 = f32[2,3,4,128,128]{4,3,2,1,0:T(8,128)} custom-call(f32[2,3,4,128,128]{4,3,2,1,0:T(8,128)} %refs_0_.1, f32[2,3,4,128,128]{4,3,2,1,0:T(8,128)} %refs_1_.1, f32[4,128,128]{2,1,0:T(8,128)} %refs_2_.1, s32[2,128]{1,0:T(2,128)} %bitcast.1, s32[2,128]{1,0:T(2,128)} %refs_4_.1), custom_call_target="tpu_custom_call" | custom-call | tf_op jit(solution)/shard_map/pallas_call | solution.py:513
  194.7 2.7 %copy.7 = f32[2,3,4,128,128]{4,3,2,1,0:T(8,128)} copy(f32[2,3,4,128,128]{4,3,2,1,0:T(8,128)} %shard_map.55) | data formatting | bytes 3145728

commit v4 on v3

--- a/solution.py
+++ b/solution.py
@@ -325,6 +325,7 @@
             gamma[p] = rate * inverse
 
     state_load.wait()
+    end = (STEPS * SWEEPS) % 2
 
     def pass_copy(source, c):
         return pltpu.make_async_remote_copy(
@@ -344,6 +345,38 @@
             delta[0, c, p + 3, inner] = value - start_state[0, c, p]
         start(lambda way: delta_copy(0, c, way))
         return 0
+
+    def coarse(s, c, p):
+        total, _ = beside(w2, (), p + 1)
+        return gamma[p + 2] * delta[s, c, p + 3, inner] + dinv_c[p + 2] * total
+
+    def coarse_before(s, c):
+        for p in range(planes + 4):
+            total, here = beside(delta, (s, c), p + 1)
+            w1[p, inner] = gamma[p] * here + dinv_c[p] * total
+        for p in range(planes + 2):
+            total, _ = beside(w1, (), p + 1)
+            w2[p, inner] = gamma[p + 1] * delta[s, c, p + 2, inner] + dinv_c[p + 1] * total
+
+    def second(c, _):
+        arrived(lambda way: delta_copy(0, c, way))
+        coarse_before(0, c)
+        for p in range(planes):
+            value = coarse(0, c, p) + v[end, place_of(0, c), p + 1, inner]
+            out[1, c, p] = value
+            delta[1, c, p + 3, inner] = value - start_state[1, c, p]
+
+        @pl.when(rank < n_tm - 1)
+        def _():
+            start(lambda way: delta_copy(1, c, way))
+
+        return 0
+
+    def by_component(first_at, past, act):
+        def one(i, _):
+            return act(lax.rem(i + 1, n_comp), 0)
+
+        lax.fori_loop(first_at, past, one, 0)
 
     def couple(landing):
         for s in range(n_slice):
@@ -396,7 +429,12 @@
             if sweep == EARLY:
                 @pl.when((rank == 0) & (step == STEPS - 1))
                 def _():
-                    lax.fori_loop(0, n_comp, first, 0)
+                    by_component(0, n_comp, first)
+
+            if sweep == SWEEPS - 1:
+                @pl.when((rank == 0) & (step == STEPS - 1))
+                def _():
+                    by_component(0, n_comp - 1, second)
 
             def tied(s, _, sweep=sweep):
                 task(step, sweep, n_free + s, True)
@@ -423,7 +461,6 @@
         return 0
 
     lax.fori_loop(0, STEPS, one_step, 0)
-    end = (STEPS * SWEEPS) % 2
 
     @pl.when(rank == n_tm - 1)
     def _():
@@ -431,39 +468,13 @@
             pass_copy(v.at[end, place_of(n_slice - 1, c), pl.ds(1, planes), inner], c).start()
             return 0
 
-        lax.fori_loop(0, n_comp, one, 0)
-
-    def coarse(s, c, p):
-        total, _ = beside(w2, (), p + 1)
-        return gamma[p + 2] * delta[s, c, p + 3, inner] + dinv_c[p + 2] * total
-
-    def coarse_before(s, c):
-        for p in range(planes + 4):
-            total, here = beside(delta, (s, c), p + 1)
-            w1[p, inner] = gamma[p] * here + dinv_c[p] * total
-        for p in range(planes + 2):
-            total, _ = beside(w1, (), p + 1)
-            w2[p, inner] = gamma[p + 1] * delta[s, c, p + 2, inner] + dinv_c[p + 1] * total
+        by_component(0, n_comp, one)
 
     @pl.when(rank > 0)
     def _():
-        lax.fori_loop(0, n_comp, first, 0)
-
-    def second(c, _):
-        arrived(lambda way: delta_copy(0, c, way))
-        coarse_before(0, c)
-        for p in range(planes):
-            value = coarse(0, c, p) + v[end, place_of(0, c), p + 1, inner]
-            out[1, c, p] = value
-            delta[1, c, p + 3, inner] = value - start_state[1, c, p]
-
-        @pl.when(rank < n_tm - 1)
-        def _():
-            start(lambda way: delta_copy(1, c, way))
-
-        return 0
-
-    lax.fori_loop(0, n_comp, second, 0)
+        by_component(0, n_comp, first)
+
+    by_component(jnp.where(rank == 0, n_comp - 1, 0), n_comp, second)
 
     @pl.when(rank < n_tm - 1)
     def _():
@@ -475,7 +486,7 @@
             pass_copy(passed.at[c], c).start()
             return 0
 
-        lax.fori_loop(0, n_comp, third, 0)
+        by_component(0, n_comp, third)
 
     for f in range(n_field):
         sent(lambda way: halo_copy(1 - end, f, way))

time: 199 us -> 199 us (level)
  no operation moved by 1% of the time
where the time goes in v4:
time: 199 us; the launch traced here: 197 us
  Pallas kernels  195 us (98%)
  local copies, waits for them, and re-layouts  2.7 us (1%)
    pallas_call x1, Pallas kernels, shards(): pl.pallas_call(body, out_shape=jax.ShapeDtypeStruct(states.shape, jnp.flo...  195 us

profile of v4, /device:TPU:13, one launch (start us, length us, event | category | flops | bytes accessed | tf_op | source)
XLA Modules:
  0.0 197.4 jit_solution(12426186278708668062)
XLA Ops:
  0.0 194.7 %shard_map.55 = f32[2,3,4,128,128]{4,3,2,1,0:T(8,128)} custom-call(f32[2,3,4,128,128]{4,3,2,1,0:T(8,128)} %refs_0_.1, f32[2,3,4,128,128]{4,3,2,1,0:T(8,128)} %refs_1_.1, f32[4,128,128]{2,1,0:T(8,128)} %refs_2_.1, s32[2,128]{1,0:T(2,128)} %bitcast.1, s32[2,128]{1,0:T(2,128)} %refs_4_.1), custom_call_target="tpu_custom_call" | custom-call | tf_op jit(solution)/shard_map/pallas_call | solution.py:524
  194.7 2.7 %copy.7 = f32[2,3,4,128,128]{4,3,2,1,0:T(8,128)} copy(f32[2,3,4,128,128]{4,3,2,1,0:T(8,128)} %shard_map.55) | data formatting | bytes 3145728

commit v5 on v4

--- a/solution.py
+++ b/solution.py
@@ -340,10 +340,10 @@
     def first(c, _):
         pass_copy(new0.at[c], c).wait_recv()
         for p in range(planes):
-            value = new0[c, p]
-            out[0, c, p] = value
-            delta[0, c, p + 3, inner] = value - start_state[0, c, p]
+            delta[0, c, p + 3, inner] = new0[c, p] - start_state[0, c, p]
         start(lambda way: delta_copy(0, c, way))
+        for p in range(planes):
+            out[0, c, p] = new0[c, p]
         return 0
 
     def coarse(s, c, p):

time: 199 us -> 199 us (level)
  no operation moved by 1% of the time
where the time goes in v5:
time: 199 us; the launch traced here: 197 us
  Pallas kernels  195 us (98%)
  local copies, waits for them, and re-layouts  2.7 us (1%)
    pallas_call x1, Pallas kernels, shards(): pl.pallas_call(body, out_shape=jax.ShapeDtypeStruct(states.shape, jnp.flo...  195 us

profile of v5, /device:TPU:13, one launch (start us, length us, event | category | flops | bytes accessed | tf_op | source)
XLA Modules:
  0.0 197.4 jit_solution(2816544585824125586)
XLA Ops:
  0.0 194.7 %shard_map.55 = f32[2,3,4,128,128]{4,3,2,1,0:T(8,128)} custom-call(f32[2,3,4,128,128]{4,3,2,1,0:T(8,128)} %refs_0_.1, f32[2,3,4,128,128]{4,3,2,1,0:T(8,128)} %refs_1_.1, f32[4,128,128]{2,1,0:T(8,128)} %refs_2_.1, s32[2,128]{1,0:T(2,128)} %bitcast.1, s32[2,128]{1,0:T(2,128)} %refs_4_.1), custom_call_target="tpu_custom_call" | custom-call | tf_op jit(solution)/shard_map/pallas_call | solution.py:524
  194.7 2.7 %copy.7 = f32[2,3,4,128,128]{4,3,2,1,0:T(8,128)} copy(f32[2,3,4,128,128]{4,3,2,1,0:T(8,128)} %shard_map.55) | data formatting | bytes 3145728
